TPU v7x, 32 devices: a whole 2x2x4 slice. The times are simulated.
32 devices in a mesh: section: 2 (over y), dp: 16 (over z, x, core).
Axes of the slice: x: 2, y: 2, z: 4, core: 2. Of those that a mesh axis runs over, the one named last changes fastest.
Arguments:
- phonemes: bfloat16 [64, 160, 256], P('dp'), may hold values from -6 to 6
- phone_lengths: int32 [64], P('dp'), may hold values from 80 to 160, as said below
- durations: int32 [64, 160], P('dp'), may hold values from 0 to 95, as said below
- pitch_bins: int32 [64, 1024], P('dp'), may hold values from 0 to 255
- energy_bins: int32 [64, 1024], P('dp'), may hold values from 0 to 255
- joint_weight: bfloat16 [2, 256, 768], P('section'), may hold values from -0.375 to 0.375
- output_weight: bfloat16 [2, 256, 256], P('section'), may hold values from -1.5 to 1.5
- widen_weight: bfloat16 [2, 2304, 1024], P('section'), may hold values from -0.125 to 0.125
- narrow_weight: bfloat16 [2, 1024, 256], P('section'), may hold values from -0.1875 to 0.1875
- block_scales: float32 [2, 2, 256], P('section'), may hold values from 0.25 to 1.75
- block_shifts: float32 [2, 2, 256], P('section'), may hold values from -3 to 3
- predictor_convs: bfloat16 [3, 2, 768, 256], replicated, may hold values from -0.21875 to 0.21875
- predictor_scales: float32 [3, 2, 256], replicated, may hold values from 0.25 to 1.75
- predictor_shifts: float32 [3, 2, 256], replicated, may hold values from -3 to 3
- predictor_outputs: float32 [3, 256], replicated, may hold values from -0.375 to 0.375
- pitch_table: bfloat16 [256, 256], replicated, may hold values from -3 to 3
- energy_table: bfloat16 [256, 256], replicated, may hold values from -3 to 3
- mel_weight: bfloat16 [256, 80], replicated, may hold values from -0.375 to 0.375
- mel_cotangent: bfloat16 [64, 1024, 80], P('dp'), may hold values from -6 to 6
- duration_cotangent: float32 [64, 160], P('dp'), may hold values from -6 to 6
- pitch_cotangent: float32 [64, 1024], P('dp'), may hold values from -6 to 6
- energy_cotangent: float32 [64, 1024], P('dp'), may hold values from -6 to 6
Outputs:
- mel_out: float32 [64, 1024, 80], P('dp', 'section')
- duration_pred: float32 [64, 160], P('dp', 'section')
- pitch_pred: float32 [64, 1024], P('dp', 'section')
- energy_pred: float32 [64, 1024], P('dp', 'section')
- input_grad: float32 [64, 160, 256], P('dp', 'section')
- grad_joint: float32 [2, 256, 768], P('section', 'dp')
- grad_output: float32 [2, 256, 256], P('section', 'dp')
- grad_widen: float32 [2, 2304, 1024], P('section', 'dp')
- grad_narrow: float32 [2, 1024, 256], P('section', 'dp')
- grad_block_scales: float32 [2, 2, 256], P('section', None, 'dp')
- grad_block_shifts: float32 [2, 2, 256], P('section', None, 'dp')
- grad_predictor_convs: float32 [3, 2, 768, 256], P(None, None, None, 'dp')
- grad_predictor_scales: float32 [3, 2, 256], P(None, None, 'dp')
- grad_predictor_shifts: float32 [3, 2, 256], P(None, None, 'dp')
- grad_predictor_outputs: float32 [3, 256], P(None, 'dp')
- grad_pitch_table: float32 [256, 256], P(None, 'dp')
- grad_energy_table: float32 [256, 256], P(None, 'dp')
- grad_mel_weight: float32 [256, 80], P('dp')
Inputs may be any that keep to these rules, and one draw needn't show every extreme that they name: `phone_lengths`: some sequence has exactly 160 phonemes. Positions at or past a sequence's phoneme count have duration 0; a sequence's durations sum to 512 to 1024, and those of the sequence with 160 phonemes to exactly 1024; some phoneme of that sequence has the largest duration.
All inputs are finite; a program needn't handle non-finite values.
Results may differ from a plain program's by a relative error of at most 0.02.
Values may be sent and summed in bfloat16 or wider, within the bound.
A program may use at most 384 MiB of HBM per device.

v0:
```python
import functools
import itertools
import math

import jax
import jax.numpy as jnp
from jax import lax
from jax.experimental import pallas as pl
from jax.experimental.pallas import tpu as pltpu
from jax.sharding import PartitionSpec as P

D = 256
HEAD = 128
FF = 1024
BINS = 256
MELS = 80
TAPS = 9
PHONES = 160
FRAMES = 1024
SLOT = 192
WIDE = TAPS * D
EPS = 1e-5
AT_VECTORS = 6 * 3 * D
AT_TABLES = AT_VECTORS + 128
AT_MEL = AT_TABLES + 2 * BINS
PACK = AT_MEL + 128
NEAR_PACK = AT_TABLES + BINS
C1 = math.sqrt(2.0 / math.pi)
C2 = C1 * 0.044715
SCALE = HEAD**-0.5
SECTION = "section"
DP = "dp"
LOG2E = math.log2(math.e)
F32 = jnp.float32
BF16 = jnp.bfloat16


def names(**kept):
    return tuple(kept)


def dot(a, b):
    return jnp.dot(a, b, preferred_element_type=F32)


def dot_nt(a, b):
    return lax.dot_general(a, b, (((1,), (1,)), ((), ())), preferred_element_type=F32)


def dot_tn(a, b):
    return lax.dot_general(a, b, (((0,), (0,)), ((), ())), preferred_element_type=F32)


def iota(shape, dim):
    return lax.broadcasted_iota(jnp.int32, shape, dim)


def gelu_pair(x):
    x2 = x * x
    h = 0.5 + 0.5 * jnp.tanh(x * (C1 + C2 * x2))
    value = x * h
    slope = h + value * (1.0 - h) * (2.0 * C1 + 6.0 * C2 * x2)
    return value, slope


def normed(r):
    mean = jnp.mean(r, axis=-1, keepdims=True)
    centred = r - mean
    rstd = lax.rsqrt(jnp.mean(centred * centred, axis=-1, keepdims=True) + EPS)
    return centred * rstd, rstd


def norm_back(t, n, rstd):
    return (
        t - jnp.mean(t, axis=-1, keepdims=True) - n * jnp.mean(t * n, axis=-1, keepdims=True)
    ) * rstd


def column_sum(x):
    return jnp.sum(x, axis=0, keepdims=True)


def aligned(i, size):
    return pl.ds(pl.multiple_of(i * size, size), size)


def each(count, body):
    def step(i, carry):
        body(i)
        return carry

    lax.fori_loop(0, count, step, 0)


class Layout:
    def __init__(self, segments, span, query):
        self.segments, self.span, self.query = segments, span, query
        self.rows = segments * span
        self.fewest = span // 2


ENC = Layout(4, SLOT, SLOT)
DEC = Layout(1, FRAMES, 256)
T = 256
AHEAD = 2


def pieces(length, size):
    return [(at, min(size, length - at)) for at in range(0, length, size)]


def block_scratch(layout, backward):
    L, S, n = layout.rows, layout.span, layout.segments
    shapes = dict(
        h_lo=pltpu.VMEM((L, D), BF16),
        joint=pltpu.VMEM((L, 3 * D), BF16),
        jointT=pltpu.VMEM((n, 3 * D, S), BF16),
        mixedT=pltpu.VMEM((n, D, S), BF16),
        first=pltpu.VMEM((L + 16, D), F32),
        cols=pltpu.VMEM((L, WIDE), BF16),
        slope=pltpu.VMEM((L, FF), F32),
        wide=pltpu.VMEM((2, T, D), F32),
        second=pltpu.VMEM((L, D), F32),
        widen=pltpu.VMEM((WIDE, FF), BF16),
        narrow=pltpu.VMEM((FF, D), BF16),
        sem=pltpu.SemaphoreType.DMA((6,)),
    )
    if backward:
        shapes.update(
            expo=pltpu.VMEM((n, 2, S, S), BF16),
            rinv=pltpu.VMEM((n, 2, 8, S), F32),
            n1=pltpu.VMEM((L, D), F32),
            r1=pltpu.VMEM((L, 1), F32),
            act=pltpu.VMEM((L, FF), BF16),
            spare=pltpu.VMEM((WIDE - 2 * L, FF), BF16),
            dnar=pltpu.VMEM((max(L, FF), D), BF16),
            dwid=pltpu.VMEM((L, FF), BF16),
            dcols=pltpu.VMEM((T + 32, WIDE), F32),
            dfirst=pltpu.VMEM((L + 16, D), F32),
            datt=pltpu.VMEM((L, D), BF16),
            dmixT=pltpu.VMEM((n, D, S), BF16),
            inner=pltpu.VMEM((n, 2, 8, S), F32),
            djointT=pltpu.VMEM((n, 3 * D, S), BF16),
            joint_turned=pltpu.VMEM((3 * D, D), BF16),
            a_joint=pltpu.VMEM((3 * D, D), F32),
            a_output=pltpu.VMEM((D, D), F32),
            a_widen=pltpu.VMEM((WIDE, FF), F32),
            a_narrow=pltpu.VMEM((FF, D), F32),
            a_vec=pltpu.VMEM((8, D), F32),
        )
    return shapes


def start_block(layout, b):
    edge = jnp.zeros((8, D), F32)
    b.first[0:8, :] = edge
    b.first[layout.rows + 8 : layout.rows + 16, :] = edge


def zero_accumulators(b, w):
    b.joint_turned[...] = w.joint[...].T
    b.a_joint[...] = jnp.zeros_like(b.a_joint)
    b.a_output[...] = jnp.zeros_like(b.a_output)
    b.a_narrow[...] = jnp.zeros_like(b.a_narrow)
    b.a_vec[...] = jnp.zeros_like(b.a_vec)

    def body(t, _):
        b.a_widen[aligned(t, D), :] = jnp.zeros((D, FF), F32)
        return 0

    lax.fori_loop(0, TAPS, body, 0)
    edge = jnp.zeros((16, WIDE), F32)
    b.dcols[0:16, :] = edge


def heads(h):
    return tuple(slice(k * D + h * HEAD, k * D + (h + 1) * HEAD) for k in range(3))


def span(start, size):
    if isinstance(start, int):
        return slice(start, start + size)
    return pl.ds(pl.multiple_of(start, math.gcd(size, 256)), size)


def tile_rows(k, extra=0, first=0):
    return pl.ds(pl.multiple_of(k * T + first, 8), T + extra)


def attention_forward(layout, b, w, counts, length):
    S, save = layout.span, hasattr(b, "expo")
    blocks = [(s, at, q) for s in range(layout.segments) for at, q in pieces(length, layout.query)]
    for s, at, q in blocks:
        rows = slice(s * S + at, s * S + at + q)
        value = dot(b.h_lo[rows, :], w.joint[...]).astype(BF16)
        b.joint[rows, :] = value
        b.jointT[s, :, at : at + q] = value.T
    chunks = pieces(length, D)
    items = [block + (h,) for block in blocks for h in range(2)]

    def score(i):
        s, at, q, h = items[i]
        query_at, key_at, _ = heads(h)
        side = slice((i % 2) * D, (i % 2) * D + q)
        top = None
        for c, size in chunks:
            scores = dot(
                b.joint[s * S + c : s * S + c + size, key_at], b.jointT[s, query_at, at : at + q]
            )
            if c + size > layout.fewest:
                scores = jnp.where(iota((size, q), 0) + c < counts[s], scores, -1e30)
            b.slope[c : c + size, side] = scores
            part = jnp.max(scores.reshape(size // 8, 8, q), axis=0)
            top = part if top is None else jnp.maximum(top, part)
        return jnp.max(top, axis=0, keepdims=True)

    tops = {0: score(0)}
    for i, (s, at, q, h) in enumerate(items):
        if i + 1 < len(items):
            tops[i + 1] = score(i + 1)
        query_at, _, value_at = heads(h)
        side = slice((i % 2) * D, (i % 2) * D + q)
        sums = mixed = None
        for c, size in chunks:
            expo = jnp.exp2((b.slope[c : c + size, side] - tops[i]) * (SCALE * LOG2E))
            part = jnp.sum(expo.reshape(size // 8, 8, q), axis=0)
            sums = part if sums is None else sums + part
            expo = expo.astype(BF16)
            if save:
                b.expo[s, h, c : c + size, at : at + q] = expo
            part = dot(b.jointT[s, value_at, c : c + size], expo)
            mixed = part if mixed is None else mixed + part
        rinv = 1.0 / column_sum(sums)
        b.mixedT[s, query_at, at : at + q] = (mixed * rinv).astype(BF16)
        if save:
            b.rinv[s, h, :, at : at + q] = jnp.broadcast_to(rinv, (8, q))
    for s, at, q in blocks:
        r0 = s * S + at
        attended = dot_tn(b.mixedT[s, :, at : at + q], w.output[...])
        n, rstd = normed(b.h_lo[r0 : r0 + q, :].astype(F32) + attended)
        keep = (iota((q, 1), 0) + at < counts[s]).astype(F32)
        b.first[r0 + 8 : r0 + 8 + q, :] = (n * w.scales[0:1, :] + w.shifts[0:1, :]) * keep
        if save:
            b.n1[r0 : r0 + q, :] = n
            b.r1[r0 : r0 + q, :] = rstd


def ffn_forward(b, w, length):
    save = hasattr(b, "expo")
    tiles = pieces(length, T)
    items = [(k, j) for k in range(len(tiles)) for j in range(4)]

    def unfold(k):
        r0, size = tiles[k]
        v = b.first[r0 : r0 + size + 16, :]
        for t in range(TAPS):
            b.cols[r0 : r0 + size, t * D : (t + 1) * D] = v[4 + t : 4 + t + size].astype(BF16)

    def widen(i):
        k, j = items[i]
        r0, size = tiles[k]
        b.wide[i % 2, 0:size, :] = dot(b.cols[r0 : r0 + size, :], b.widen[:, j * D : (j + 1) * D])

    unfold(0)
    widen(0)
    for i, (k, j) in enumerate(items):
        if j == 1 and k + 1 < len(tiles):
            unfold(k + 1)
        if i + 1 < len(items):
            widen(i + 1)
        r0, size = tiles[k]
        rows, at = slice(r0, r0 + size), slice(j * D, (j + 1) * D)
        value, slope = gelu_pair(b.wide[i % 2, 0:size, :])
        value = value.astype(BF16)
        if save:
            b.act[rows, at] = value
            b.slope[rows, at] = slope
        narrowed = dot(value, b.narrow[at, :])
        before = b.second[rows, :] if j else b.first[r0 + 8 : r0 + 8 + size, :]
        b.second[rows, :] = before + narrowed


def ffn_backward(b, w, length):
    b.dfirst[0 : length + 16, :] = jnp.zeros((length + 16, D), F32)
    for r0, size in pieces(length, T):
        rows = slice(r0, r0 + size)
        b.dcols[16 + size : 32 + size, :] = jnp.zeros((16, WIDE), F32)
        for j in range(4):
            at = slice(j * D, (j + 1) * D)
            b.dwid[rows, at] = (
                dot_nt(b.dnar[rows, :], b.narrow[at, :]) * b.slope[rows, at]
            ).astype(BF16)
        for t in range(TAPS):
            at = slice(t * D, (t + 1) * D)
            b.dcols[16 : 16 + size, at] = dot_nt(b.dwid[rows, :], b.widen[at, :])
        total = b.dcols[12 : 28 + size, 0:D]
        for t in range(1, TAPS):
            total = total + b.dcols[12 - t : 28 - t + size, t * D : (t + 1) * D]
        b.dfirst[r0 : r0 + size + 16, :] += total
        b.dfirst[r0 + 8 : r0 + 8 + size, :] += b.second[rows, :]


def ffn_weight_grads(b, length):
    def widen(t, _):
        at = aligned(t, 3 * D)
        b.a_widen[at, :] += dot_tn(b.cols[0:length, at], b.dwid[0:length, :])
        return 0

    lax.fori_loop(0, 3, widen, 0)
    b.a_narrow[...] += dot_tn(b.act[0:length, :], b.dnar[0:length, :])


def attention_backward(layout, b, w, counts, length, finish):
    S = layout.span
    blocks = [(s, at, q) for s in range(layout.segments) for at, q in pieces(length, layout.query)]
    chunks = pieces(length, D)
    for s, at, q in blocks:
        r0 = s * S + at
        rows, pad_rows, lanes = slice(r0, r0 + q), slice(r0 + 8, r0 + 8 + q), slice(at, at + q)
        keep = (iota((q, 1), 0) + at < counts[s]).astype(F32)
        dy = b.dfirst[pad_rows, :] * keep
        n = b.n1[rows, :]
        b.a_vec[0:1, :] += column_sum(dy * n)
        b.a_vec[1:2, :] += column_sum(dy)
        dsum = norm_back(dy * w.scales[0:1, :], n, b.r1[rows, :])
        b.dfirst[pad_rows, :] = dsum
        datt = dsum.astype(BF16)
        b.datt[rows, :] = datt
        dmix = dot_nt(w.output[...], datt)
        for h in range(2):
            head = heads(h)[0]
            part = (dmix[head, :] * b.rinv[s, h, 0:1, lanes]).astype(BF16)
            b.dmixT[s, head, lanes] = part
            inner = column_sum(part.astype(F32) * b.mixedT[s, head, lanes].astype(F32))
            b.inner[s, h, :, lanes] = jnp.broadcast_to(inner, (8, q))
    items = [block + (h,) for block in blocks for h in range(2)]

    def score(i):
        s, at, q, h = items[i]
        side = slice((i % 2) * D, (i % 2) * D + q)
        b.slope[0:length, side] = dot(
            b.joint[s * S : s * S + length, heads(h)[2]], b.dmixT[s, heads(h)[0], at : at + q]
        )

    score(0)
    for i, (s, at, q, h) in enumerate(items):
        if i + 1 < len(items):
            score(i + 1)
        query_at, key_at, _ = heads(h)
        lanes, side = slice(at, at + q), slice((i % 2) * D, (i % 2) * D + q)
        dquery = None
        for c, size in chunks:
            expo = b.expo[s, h, c : c + size, lanes].astype(F32)
            ds = expo * (b.slope[c : c + size, side] - b.inner[s, h, 0:1, lanes])
            ds = ds.astype(BF16)
            part = dot(b.jointT[s, key_at, c : c + size], ds)
            dquery = part if dquery is None else dquery + part
            b.cols[s * S + at : s * S + at + q, h * FRAMES + c : h * FRAMES + c + size] = ds.T
        b.djointT[s, query_at, lanes] = (dquery * SCALE).astype(BF16)
    for s in range(layout.segments):
        rows = slice(s * S, s * S + length)
        for h in range(2):
            query_at, key_at, value_at = heads(h)
            for c, size in chunks:
                lanes = slice(c, c + size)
                dkey = dot(
                    b.jointT[s, query_at, 0:length],
                    b.cols[rows, h * FRAMES + c : h * FRAMES + c + size],
                )
                b.djointT[s, key_at, lanes] = (dkey * SCALE).astype(BF16)
                dvalue = dot_nt(b.dmixT[s, query_at, 0:length], b.expo[s, h, lanes, 0:length])
                b.djointT[s, value_at, lanes] = dvalue.astype(BF16)
        b.a_output[...] += dot(b.mixedT[s, :, 0:length], b.datt[rows, :])
        b.a_joint[...] += dot(b.djointT[s, :, 0:length], b.h_lo[rows, :])
    for s, at, q in blocks:
        dh = dot_tn(b.djointT[s, :, at : at + q], b.joint_turned[...])
        finish(s, at, q, dh + b.dfirst[s * S + at + 8 : s * S + at + 8 + q, :])


def second_norm_back(b, w, r0, size, dy, n, rstd):
    b.a_vec[2:3, :] += column_sum(dy * n)
    b.a_vec[3:4, :] += column_sum(dy)
    dsecond = norm_back(dy * w.scales[1:2, :], n, rstd)
    b.second[r0 : r0 + size, :] = dsecond
    b.dnar[r0 : r0 + size, :] = dsecond.astype(BF16)


class Refs:
    def __init__(self, names, refs):
        for name, ref in zip(names, refs):
            setattr(self, name, ref)


WEIGHTS = names(joint=1, output=1, widen_far=1, narrow_far=1, scales=1, shifts=1)
FAR = names(w_widen_far=1, w_narrow_far=1, g_widen=1, g_narrow=1)


def send_large_grads(b, o):
    b.dnar[0:FF, :] = b.a_narrow[...].astype(BF16)
    pltpu.make_async_copy(b.dnar.at[pl.ds(0, FF)], o.g_narrow, b.sem.at[2]).start()
    at = 0
    for k, (buffer, size) in enumerate(large_parts(b)):
        buffer[0:size, :] = b.a_widen[at : at + size, :].astype(BF16)
        pltpu.make_async_copy(
            buffer.at[pl.ds(0, size)], o.g_widen.at[pl.ds(at, size)], b.sem.at[3 + k]
        ).start()
        at += size


def large_parts(b):
    size = b.act.shape[0]
    left = WIDE - 2 * size
    return ((b.act, size), (b.dwid, size), (b.spare, left))


def store_block_grads(b, o):
    o.g_joint[...] = b.a_joint[...].T.astype(BF16)
    o.g_output[...] = b.a_output[...].astype(BF16)
    rows = jnp.concatenate([b.a_vec[...], jnp.zeros((120, D), F32)], axis=0)
    o.g_vec[...] = rows.T.astype(BF16)
    pltpu.make_async_copy(b.dnar.at[pl.ds(0, FF)], o.g_narrow, b.sem.at[2]).wait()
    at = 0
    for k, (buffer, size) in enumerate(large_parts(b)):
        pltpu.make_async_copy(
            buffer.at[pl.ds(0, size)], o.g_widen.at[pl.ds(at, size)], b.sem.at[3 + k]
        ).wait()
        at += size


def start_weights(b, w):
    pltpu.make_async_copy(w.widen_far, b.widen, b.sem.at[0]).start()
    pltpu.make_async_copy(w.narrow_far, b.narrow, b.sem.at[1]).start()


def wait_weights(b, w):
    pltpu.make_async_copy(w.widen_far, b.widen, b.sem.at[0]).wait()
    pltpu.make_async_copy(w.narrow_far, b.narrow, b.sem.at[1]).wait()


GRADS = dict(
    g_joint=((D, 3 * D), BF16),
    g_output=((D, D), BF16),
    g_widen=((WIDE, FF), BF16),
    g_narrow=((FF, D), BF16),
    g_vec=((D, 128), BF16),
)


def expansion(start, stop, first_row, size):
    row = iota((size, 256), 0) + first_row
    return ((row >= start) & (row < stop)).astype(F32).astype(BF16)


def hot_columns(bins, count, first_lane, size):
    live = iota((1, size), 1) + first_lane < count
    return ((iota((BINS, size), 0) == bins) & live).astype(F32).astype(BF16)


def span_ends(durations):
    upper = (iota((256, 256), 0) <= iota((256, 256), 1)).astype(F32).astype(BF16)
    return dot(durations.astype(F32).astype(BF16), upper).astype(jnp.int32)


def decoder_kernel(sequences, r):
    b, w, o = r, Refs(WEIGHTS, [getattr(r, "w_" + n) for n in WEIGHTS]), r
    layout = DEC
    start_weights(b, w)
    zero_accumulators(b, w)
    start_block(layout, b)
    r.a_mel[...] = jnp.zeros_like(r.a_mel)
    r.a_table[...] = jnp.zeros_like(r.a_table)
    r.durations_pad[...] = jnp.zeros_like(r.durations_pad)
    r.durations_pad[0:sequences, 0:PHONES] = r.durations[...]
    stop = span_ends(r.durations_pad[...])
    r.stop[...] = stop
    r.start[...] = stop - r.durations_pad[...]
    r.encoded_pad[...] = jnp.zeros_like(r.encoded_pad)

    def sequence(s, length):
        count = r.frames[s]
        counts = [count]
        r.encoded_pad[0:PHONES, :] = r.arrived[s]
        start, stop = r.start[pl.ds(s, 1), :], r.stop[pl.ds(s, 1), :]
        tiles = pieces(length, T)
        for r0, size in tiles:
            rows = slice(r0, r0 + size)
            expand = expansion(start, stop, r0, size)
            r.expand[rows, :] = expand
            hot_p = hot_columns(r.pitch_bins[pl.ds(s, 1), rows], count, r0, size)
            hot_e = hot_columns(r.energy_bins[pl.ds(s, 1), rows], count, r0, size)
            r.hot[0:BINS, rows] = hot_p
            r.hot[BINS:, rows] = hot_e
            adapted = dot(expand, r.encoded_pad[...])
            adapted = adapted + dot_tn(hot_p, r.pitch_table[...])
            adapted = adapted + dot_tn(hot_e, r.energy_table[...])
            b.h_lo[rows, :] = adapted.astype(BF16)
        attention_forward(layout, b, w, counts, length)
        b.first[length + 8 : length + 16, :] = jnp.zeros((8, D), F32)
        pl.when(s == 0)(lambda: wait_weights(b, w))
        ffn_forward(b, w, length)
        for r0, size in tiles:
            rows = slice(r0, r0 + size)
            n, rstd = normed(b.second[rows, :])
            keep = (iota((size, 1), 0) + r0 < count).astype(F32)
            decoded = ((n * w.scales[1:2, :] + w.shifts[1:2, :]) * keep).astype(BF16)
            spectrum = dot_nt(r.mel_turned[...], decoded)
            if r0 < FRAMES // 2:
                o.mel_away[s, :, rows] = spectrum.astype(BF16)
            else:
                o.mel_own[s, :, r0 - FRAMES // 2 : r0 - FRAMES // 2 + size] = spectrum
            cotangent = r.mel_cotangent[s, :, rows]
            r.a_mel[...] += dot(cotangent, decoded)
            dy = dot_tn(cotangent, r.mel_turned[...]) * keep
            second_norm_back(b, w, r0, size, dy, n, rstd)
        ffn_backward(b, w, length)
        ffn_weight_grads(b, length)
        pl.when(s == sequences - 1)(lambda: send_large_grads(b, o))

        def finish(_, at, q, dh):
            b.datt[at : at + q, :] = dh.astype(BF16)

        attention_backward(layout, b, w, counts, length, finish)
        dadapted = b.datt[0:length, :]
        r.a_table[...] += dot(r.hot[:, 0:length], dadapted)
        o.dsent[s] = dot_tn(r.expand[0:length, :], dadapted)[0:PHONES].astype(BF16)

    def one(s):
        sequence(s, FRAMES)

    each(sequences, one)
    store_block_grads(b, o)
    r.pack_far[:, 0 : 2 * BINS] = r.a_table[...].T.astype(BF16)
    r.pack_far[:, 2 * BINS :] = jnp.zeros((D, 128), BF16)
    r.pack_far[:, 2 * BINS : 2 * BINS + MELS] = r.a_mel[...].T.astype(BF16)


def section_call(name, inputs, outputs, branches, smem=(), kept=()):
    shapes = {n: (a.shape, a.dtype) for n, a in inputs.items()}

    def kernel(*refs):
        place = dict(zip(inputs, refs))
        target = dict(zip(outputs, refs[len(inputs) :]))

        def run(body, ins, outs, scratch):
            near_ins = [n for n in ins if n not in FAR and n not in smem]
            near_outs = [n for n in outs if n not in FAR]
            local = {n: pltpu.VMEM(*shapes[n]) for n in near_ins}
            local.update({n: pltpu.VMEM(*outputs[n]) for n in near_outs})
            local.update(scratch)
            local.update(
                sem_in=pltpu.SemaphoreType.DMA((len(near_ins),)),
                sem_out=pltpu.SemaphoreType.DMA((len(near_outs),)),
            )

            def scoped(*values):
                r = Refs(list(local), values)
                for n in ins:
                    if n not in near_ins:
                        setattr(r, n, place[n])
                for n in outs:
                    if n not in near_outs:
                        setattr(r, n, target[n])
                copies = [
                    pltpu.make_async_copy(place[n], getattr(r, n), r.sem_in.at[k])
                    for k, n in enumerate(near_ins)
                ]
                for copy in copies:
                    copy.start()
                for copy in copies:
                    copy.wait()
                body(r)
                copies = [
                    pltpu.make_async_copy(getattr(r, n), target[n], r.sem_out.at[k])
                    for k, n in enumerate(near_outs)
                ]
                for copy in copies:
                    copy.start()
                for copy in copies:
                    copy.wait()

            pl.run_scoped(scoped, *local.values())

        for section, branch in enumerate(branches):
            if branch is not None:
                here = (lax.axis_index(SECTION) == section).astype(jnp.int32)
                each(here, lambda _: run(*branch))

    index_in = list(inputs)
    return pl.pallas_call(
        kernel,
        name=name,
        in_specs=[
            pl.BlockSpec(memory_space=pltpu.SMEM if n in smem else pl.ANY) for n in inputs
        ],
        out_specs=[pl.BlockSpec(memory_space=pl.ANY)] * len(outputs),
        out_shape=[jax.ShapeDtypeStruct(*outputs[n]) for n in outputs],
        input_output_aliases={index_in.index(n): k for k, n in enumerate(outputs) if n in kept},
        compiler_params=pltpu.CompilerParams(vmem_limit_bytes=61 * 2**20),
    )(*inputs.values())


W_NAMES = tuple("w_" + n for n in WEIGHTS)
G_NAMES = tuple(GRADS)


def decoder_branch(sequences):
    scratch = dict(
        block_scratch(DEC, True),
        a_mel=pltpu.VMEM((MELS, D), F32),
        a_table=pltpu.VMEM((2 * BINS, D), F32),
        durations_pad=pltpu.VMEM((8, 256), jnp.int32),
        start=pltpu.VMEM((8, 256), jnp.int32),
        stop=pltpu.VMEM((8, 256), jnp.int32),
        encoded_pad=pltpu.VMEM((256, D), BF16),
        expand=pltpu.VMEM((FRAMES, 256), BF16),
        hot=pltpu.VMEM((2 * BINS, FRAMES), BF16),
    )
    ins = names(frames=1, arrived=1, durations=1, pitch_bins=1, energy_bins=1, pitch_table=1,
                energy_table=1, mel_turned=1, mel_cotangent=1)
    outs = names(mel_own=1, mel_away=1, dsent=1, pack_far=1)
    return functools.partial(decoder_kernel, sequences), ins + W_NAMES, outs + G_NAMES, scratch


def load_segments(b, phonemes):
    b.h_lo[...] = jnp.zeros_like(b.h_lo)
    for s in range(ENC.segments):
        b.h_lo[s * SLOT : s * SLOT + PHONES, :] = phonemes[s]


def slot_keep(counts, r0, size):
    row = iota((size, 1), 0) + r0
    kept = row < counts[0]
    for s in range(1, ENC.segments):
        kept = kept | ((row >= s * SLOT) & (row < s * SLOT + counts[s]))
    return kept.astype(F32)


def encoder_forward_kernel(r):
    b, w = r, Refs(WEIGHTS, [getattr(r, "w_" + n) for n in WEIGHTS])
    start_weights(b, w)
    counts = [r.counts[s] for s in range(ENC.segments)]
    start_block(ENC, b)
    load_segments(b, r.phonemes)
    attention_forward(ENC, b, w, counts, SLOT)
    wait_weights(b, w)
    ffn_forward(b, w, ENC.rows)
    for r0, size in pieces(ENC.rows, T):
        n, _ = normed(b.second[r0 : r0 + size, :])
        encoded = (n * w.scales[1:2, :] + w.shifts[1:2, :]) * slot_keep(counts, r0, size)
        b.second[r0 : r0 + size, :] = encoded
    for s in range(ENC.segments):
        encoded = b.second[s * SLOT : s * SLOT + PHONES, :]
        r.encoded[s] = encoded
        r.encoded_lo[s] = encoded.astype(BF16)


def encoder_backward_kernel(r):
    b, w, o = r, Refs(WEIGHTS, [getattr(r, "w_" + n) for n in WEIGHTS]), r
    start_weights(b, w)
    counts = [r.counts[s] for s in range(ENC.segments)]
    zero_accumulators(b, w)
    start_block(ENC, b)
    load_segments(b, r.phonemes)
    attention_forward(ENC, b, w, counts, SLOT)
    wait_weights(b, w)
    ffn_forward(b, w, ENC.rows)
    b.n1_grad[...] = jnp.zeros_like(b.n1_grad)
    for s in range(ENC.segments):
        b.n1_grad[s * SLOT : s * SLOT + PHONES, :] = r.grad_near[s] + r.grad_far[s].astype(F32)
    for r0, size in pieces(ENC.rows, T):
        n, rstd = normed(b.second[r0 : r0 + size, :])
        dy = b.n1_grad[r0 : r0 + size, :] * slot_keep(counts, r0, size)
        second_norm_back(b, w, r0, size, dy, n, rstd)
    ffn_backward(b, w, ENC.rows)
    ffn_weight_grads(b, ENC.rows)
    send_large_grads(b, o)

    def finish(s, at, q, dh):
        o.input_own[s] = dh[0 : PHONES // 2]
        o.input_away[s] = dh[PHONES // 2 : PHONES].astype(BF16)

    attention_backward(ENC, b, w, counts, SLOT, finish)
    store_block_grads(b, o)


def encoder_forward_branch():
    return (
        encoder_forward_kernel,
        names(counts=1, phonemes=1) + W_NAMES,
        names(encoded=1, encoded_lo=1),
        block_scratch(ENC, False),
    )


def encoder_backward_branch():
    return (
        encoder_backward_kernel,
        names(counts=1, phonemes=1, grad_near=1, grad_far=1) + W_NAMES,
        names(input_own=1, input_away=1) + G_NAMES,
        dict(block_scratch(ENC, True), n1_grad=pltpu.VMEM((ENC.rows, D), F32)),
    )


def halves(x):
    high = x.astype(BF16)
    return high, (x - high.astype(F32)).astype(BF16)


def predict(r, p, rows, keep, keep_row, hidden, cotangent, estimate):
    tiles = rows // T
    conv_a, conv_b = r.convs.at[p, 0], r.convs.at[p, 1]
    scale_a, scale_b = r.scales[p, 0:1, :], r.scales[p, 1:2, :]
    shift_a, shift_b = r.shifts[p, 0:1, :], r.shifts[p, 1:2, :]
    readout = r.readouts[pl.ds(p, 1), :]
    edge = jnp.zeros((8, D), F32)
    r.after[0:8, :] = edge
    r.after[rows + 8 : rows + 16, :] = edge

    def unfold(source, target, k):
        v = source[tile_rows(k, 16), :]
        for t in range(3):
            target[tile_rows(k), t * D : (t + 1) * D] = v[7 + t : 7 + t + T].astype(BF16)

    def fold(target, gradient, conv, k):
        r.dcols3[16 : 16 + T, :] = dot_nt(gradient, conv[...])
        total = r.dcols3[9 : 25 + T, 0:D]
        for t in range(1, 3):
            total = total + r.dcols3[9 - t : 25 - t + T, t * D : (t + 1) * D]
        target[tile_rows(k, 16), :] += total

    def clear(target):
        def body(k):
            target[tile_rows(k), :] = jnp.zeros((T, D), F32)

        each(tiles, body)
        target[rows : rows + 16, :] = jnp.zeros((16, D), F32)

    def first_half(k):
        at = tile_rows(k)
        unfold(hidden, r.cols_a, k)
        value, slope = gelu_pair(dot(r.cols_a[at, :], conv_a[...]))
        n, rstd = normed(value)
        r.slope_a[at, :] = slope
        r.norm_a[at, :] = n
        r.rstd_a[at, :] = rstd
        r.after[tile_rows(k, 0, 8), :] = (n * scale_a + shift_a) * keep(k * T, T)

    each(tiles, first_half)
    clear(r.dafter)
    weighted = readout * scale_b
    weighted_mean = jnp.mean(weighted, axis=1, keepdims=True)
    high, low = halves(readout)
    row = iota((16, D), 0)
    two = jnp.where(row == 0, high.astype(F32), jnp.where(row == 1, low.astype(F32), 0.0))
    two = two.astype(BF16)

    def second_half(k):
        at = span(k * T, T)
        unfold(r.after, r.cols_b, k)
        value, slope = gelu_pair(dot(r.cols_b[at, :], conv_b[...]))
        n, rstd = normed(value)
        after = n * scale_b + shift_b
        high, low = halves(after)
        with_high, with_low = dot_nt(two, high), dot_nt(two, low)
        guess = with_high[0:1] + with_high[1:2] + with_low[0:1]
        estimate[:, at] = guess * keep_row(k * T, T)
        column = jnp.broadcast_to(cotangent[:, at], (128, T)).T
        column = jnp.concatenate([column, column], axis=1) * keep(k * T, T)
        r.a_vec[p, 2:3, :] += readout * column_sum(column * n)
        r.a_vec[p, 3:4, :] += readout * column_sum(column)
        r.a_vec[p, 4:5, :] += column_sum(column * after)
        inner = jnp.mean(weighted * n, axis=1, keepdims=True)
        gradient = (column * (weighted - weighted_mean - n * inner) * rstd * slope).astype(BF16)
        r.grad_b[at, :] = gradient
        fold(r.dafter, gradient, conv_b, k)

    each(tiles, second_half)
    clear(hidden)

    def back(k):
        at = tile_rows(k)
        dy = r.dafter[tile_rows(k, 0, 8), :] * keep(k * T, T)
        n = r.norm_a[at, :]
        r.a_vec[p, 0:1, :] += column_sum(dy * n)
        r.a_vec[p, 1:2, :] += column_sum(dy)
        gradient = norm_back(dy * scale_a, n, r.rstd_a[at, :]) * r.slope_a[at, :]
        gradient = gradient.astype(BF16)
        r.grad_a[at, :] = gradient
        fold(hidden, gradient, conv_a, k)

    each(tiles, back)
    r.a_conv[p, 0] += dot_tn(r.grad_a[0:rows, :], r.cols_a[0:rows, :])
    r.a_conv[p, 1] += dot_tn(r.grad_b[0:rows, :], r.cols_b[0:rows, :])


def predictor_kernel(sequences, r):
    r.a_conv[...] = jnp.zeros_like(r.a_conv)
    r.a_vec[...] = jnp.zeros_like(r.a_vec)
    r.a_table[...] = jnp.zeros_like(r.a_table)
    r.dcols3[0:16, :] = jnp.zeros((16, 3 * D), F32)
    r.dcols3[16 + T :, :] = jnp.zeros((16, 3 * D), F32)
    r.durations_pad[...] = jnp.zeros_like(r.durations_pad)
    r.durations_pad[0:sequences, 0:PHONES] = r.durations[...]
    stop = span_ends(r.durations_pad[...])
    r.stop[...] = stop
    r.start[...] = stop - r.durations_pad[...]
    counts = [r.counts[s] for s in range(sequences)]
    slots = sequences * SLOT
    r.hidden[0, 0 : slots + 16, :] = jnp.zeros((slots + 16, D), F32)
    for s in range(sequences):
        r.hidden[0, s * SLOT + 8 : s * SLOT + 8 + PHONES, :] = r.encoded[s]

    def keep_slots(r0, size):
        return slot_keep(counts, r0, size)

    def keep_slots_row(r0, size):
        lane = iota((1, size), 1) + r0
        kept = lane < counts[0]
        for s in range(1, sequences):
            kept = kept | ((lane >= s * SLOT) & (lane < s * SLOT + counts[s]))
        return kept.astype(F32)

    predict(
        r, 0, slots, keep_slots, keep_slots_row, r.hidden.at[0], r.cot_duration, r.duration_pred
    )
    for s in range(sequences):
        r.dencoded[s] = r.hidden[0, s * SLOT + 8 : s * SLOT + 8 + PHONES, :]
    r.encoded_high[...] = jnp.zeros_like(r.encoded_high)
    r.encoded_low[...] = jnp.zeros_like(r.encoded_low)

    def one(s):
        count = r.frames[s]
        high, low = halves(r.encoded[s])
        r.encoded_high[0:PHONES, :] = high
        r.encoded_low[0:PHONES, :] = low
        start, stop = r.start[pl.ds(s, 1), :], r.stop[pl.ds(s, 1), :]
        edge = jnp.zeros((8, D), F32)
        for k in range(2):
            r.hidden[k, 0:8, :] = edge
            r.hidden[k, FRAMES + 8 : FRAMES + 16, :] = edge

        def embed(k):
            at = span(k * T, T)
            expand = expansion(start, stop, k * T, T)
            r.expand[at, :] = expand
            hot = hot_columns(r.pitch_bins[pl.ds(s, 1), at], count, k * T, T)
            r.hot[:, at] = hot
            frames = dot(expand, r.encoded_high[...]) + dot(expand, r.encoded_low[...])
            r.hidden[0, tile_rows(k, 0, 8), :] = frames
            pitched = frames + dot_tn(hot, r.pitch_table[...])
            r.hidden[1, tile_rows(k, 0, 8), :] = pitched

        each(FRAMES // T, embed)

        def keep(r0, size):
            return (iota((size, 1), 0) + r0 < count).astype(F32)

        def keep_row(r0, size):
            return (iota((1, size), 1) + r0 < count).astype(F32)

        def both(k):
            line = pl.ds(k * sequences + s, 1)
            predict(
                r, k + 1, FRAMES, keep, keep_row, r.hidden.at[k],
                r.cot_frames.at[line], r.frame_preds.at[line],
            )

        each(2, both)
        high, low = halves(r.hidden[1, 8 : FRAMES + 8, :])
        r.a_table[...] += dot(r.hot[...], high) + dot(r.hot[...], low)
        high, low = halves(r.hidden[0, 8 : FRAMES + 8, :] + r.hidden[1, 8 : FRAMES + 8, :])
        dencoded = dot_tn(r.expand[...], high) + dot_tn(r.expand[...], low)
        r.dencoded[s] = r.dencoded[s] + dencoded[0:PHONES]

    each(sequences, one)
    for p in range(3):
        for k in range(2):
            at = (2 * p + k) * 3 * D
            r.pack[:, at : at + 3 * D] = r.a_conv[p, k].astype(BF16)
    rows = jnp.concatenate([r.a_vec[p] for p in range(3)] + [jnp.zeros((104, D), F32)], axis=0)
    r.pack[:, AT_VECTORS:AT_TABLES] = rows.T.astype(BF16)
    r.pack[:, AT_TABLES : AT_TABLES + BINS] = r.a_table[...].T.astype(BF16)


def predictors_branch(sequences):
    return (
        functools.partial(predictor_kernel, sequences),
        names(frames=1, counts=1, encoded=1, durations=1, pitch_bins=1, convs=1, scales=1,
              shifts=1, readouts=1, pitch_table=1, cot_duration=1, cot_frames=1),
        names(duration_pred=1, frame_preds=1, dencoded=1, pack=1),
        dict(
            a_conv=pltpu.VMEM((3, 2, D, 3 * D), F32),
            a_vec=pltpu.VMEM((3, 8, D), F32),
            a_table=pltpu.VMEM((BINS, D), F32),
            durations_pad=pltpu.VMEM((8, 256), jnp.int32),
            start=pltpu.VMEM((8, 256), jnp.int32),
            stop=pltpu.VMEM((8, 256), jnp.int32),
            encoded_high=pltpu.VMEM((256, D), BF16),
            encoded_low=pltpu.VMEM((256, D), BF16),
            expand=pltpu.VMEM((FRAMES, 256), BF16),
            hot=pltpu.VMEM((BINS, FRAMES), BF16),
            hidden=pltpu.VMEM((2, FRAMES + 16, D), F32),
            after=pltpu.VMEM((FRAMES + 16, D), F32),
            dafter=pltpu.VMEM((FRAMES + 16, D), F32),
            cols_a=pltpu.VMEM((FRAMES, 3 * D), BF16),
            cols_b=pltpu.VMEM((FRAMES, 3 * D), BF16),
            slope_a=pltpu.VMEM((FRAMES, D), F32),
            norm_a=pltpu.VMEM((FRAMES, D), F32),
            rstd_a=pltpu.VMEM((FRAMES, 1), F32),
            grad_a=pltpu.VMEM((FRAMES, D), BF16),
            grad_b=pltpu.VMEM((FRAMES, D), BF16),
            dcols3=pltpu.VMEM((T + 32, 3 * D), F32),
        ),
    )


def swapped(array):
    return lax.ppermute(array, SECTION, [(0, 1), (1, 0)])


def scattered_anyhow(arrays):
    ways = lax.axis_size(DP)
    shares = [a.shape[0] // ways for a in arrays]
    flat = jnp.concatenate([a.reshape(ways, -1) for a in arrays], axis=1)
    flat = lax.psum_scatter(flat, DP, scatter_dimension=0, tiled=True)[0]
    out, at = [], 0
    for a, share in zip(arrays, shares):
        size = share * a.shape[1]
        out.append(flat[at : at + size].reshape(share, a.shape[1]).astype(F32))
        at += size
    return out


def scatter_kernel(steps, cuts, count, lists, trades, *refs):
    n, m = len(cuts), len(trades)
    given = max(m - 1, 0)
    sources, refs = refs[:count], refs[count:]
    traded, refs = refs[:given], refs[given:]
    outs, refs = refs[:count], refs[count:]
    arrived, refs = refs[:m], refs[m:]
    mine, landed = refs[:n], refs[n : n * (1 + steps)]
    load_sem, send_sem, recv_sem, *rest = refs[n * (1 + steps) :]
    if m:
        rounded, trade_send, trade_recv = rest
        traded = traded + (rounded,)
    me = lax.axis_index(DP)
    bits = [lax.rem(lax.div(me, 1 << k), 2) for k in range(steps)]
    partners = [me + (1 << k) * (1 - 2 * bits[k]) for k in range(steps)]
    def trade(i):
        return pltpu.make_async_remote_copy(
            src_ref=traded[i],
            dst_ref=arrived[i],
            send_sem=trade_send.at[i],
            recv_sem=trade_recv.at[i],
            device_id={SECTION: 1 - lax.axis_index(SECTION)},
            device_id_type=pl.DeviceIdType.MESH,
        )

    def every(k):
        return (slice(None),) * (steps - 1 - k)

    def source(i, bit):
        array, first, size = cuts[i]
        return sources[array].at[every(0) + (bit, slice(None), pl.ds(first, size))]

    def load(i):
        return pltpu.make_async_copy(source(i, bits[0]), mine[i], load_sem.at[i])

    def copy(i, k):
        if k == 0:
            out = source(i, 1 - bits[0])
        else:
            out = landed[i * steps + k - 1].at[every(k) + (1 - bits[k],)]
        return pltpu.make_async_remote_copy(
            src_ref=out,
            dst_ref=landed[i * steps + k],
            send_sem=send_sem.at[i, k],
            recv_sem=recv_sem.at[i, k],
            device_id={DP: partners[k]},
            device_id_type=pl.DeviceIdType.MESH,
        )

    def finish(i, k):
        copy(i, k).wait_recv()
        if k == 0:
            load(i).wait()
        there = landed[i * steps + k]
        for index in itertools.product(range(2), repeat=steps - 1 - k):
            if k == 0:
                stayed = mine[i][index]
            else:
                stayed = landed[i * steps + k - 1][index + (bits[k],)]
            total = there[index].astype(F32) + stayed.astype(F32)
            if k == steps - 1:
                array, first, size = cuts[i]
                outs[array][:, first : first + size] = total
            else:
                there[index] = total.astype(BF16)
        if k < steps - 1:
            copy(i, k + 1).start()

    def begin(i):
        copy(i, 0).start()
        load(i).start()

    def run(section, chosen):
        barrier = pltpu.get_barrier_semaphore()
        for partner in partners:
            pl.semaphore_signal(
                barrier, inc=1, device_id={DP: partner}, device_id_type=pl.DeviceIdType.MESH
            )
        if m:
            pl.semaphore_signal(
                barrier,
                inc=1,
                device_id={SECTION: 1 - lax.axis_index(SECTION)},
                device_id_type=pl.DeviceIdType.MESH,
            )
        pl.semaphore_wait(barrier, steps + (1 if m else 0))
        size = len(chosen)
        for i in range(given):
            if trades[i] == section:
                trade(i).start()
        last = [x for x, i in enumerate(chosen) if cuts[i][0] == count - 1]
        for turn in range(-AHEAD, size + steps - 1):
            if turn + AHEAD < size:
                begin(chosen[turn + AHEAD])
            for k in range(steps):
                at = turn - k
                if 0 <= at < size:
                    finish(chosen[at], k)
                    if m and trades[-1] == section and k == steps - 1 and at == last[-1]:
                        rounded[...] = outs[count - 1][...].astype(BF16)
                        trade(m - 1).start()
        for i in chosen:
            for k in range(steps):
                copy(i, k).wait_send()
        for i in range(m):
            if trades[i] == section:
                trade(i).wait_send()
            else:
                trade(i).wait_recv()

    for section, chosen in enumerate(lists):
        if chosen:
            here = (lax.axis_index(SECTION) == section).astype(jnp.int32)
            each(here, functools.partial(one_time, run, section, chosen))


def one_time(run, section, chosen, _):
    run(section, chosen)


def scattered(arrays, name, collective, width, parts, traded=(), trades=()):
    ways = lax.axis_size(DP)
    steps = ways.bit_length() - 1
    if ways != 1 << steps or any(a.shape[0] // ways % 16 for a in arrays):
        sums = scattered_anyhow(arrays)
        traded = [*traded, sums[-1].astype(BF16)] if trades else []
        return sums + [
            lax.ppermute(a, SECTION, [(s, 1 - s)]) for a, s in zip(traded, trades)
        ]
    shares = [a.shape[0] // ways for a in arrays]
    cuts = [
        (k, at, size)
        for k, a in enumerate(arrays)
        for at, size in pieces(a.shape[1], width if a.shape[0] > 1024 else 768)
    ]
    lists = [[i for k in part for i, cut in enumerate(cuts) if cut[0] == k] for part in parts]
    landed = [
        pltpu.VMEM((2,) * (steps - 1 - k) + (shares[array], size), BF16)
        for array, _, size in cuts
        for k in range(steps)
    ]
    mine = [pltpu.VMEM((2,) * (steps - 1) + (shares[array], size), BF16) for array, _, size in cuts]
    scratch = [
        *mine,
        *landed,
        pltpu.SemaphoreType.DMA((len(cuts),)),
        pltpu.SemaphoreType.DMA((len(cuts), steps)),
        pltpu.SemaphoreType.DMA((len(cuts), steps)),
    ]
    outs = [jax.ShapeDtypeStruct((share, a.shape[1]), F32) for share, a in zip(shares, arrays)]
    far, near = pl.BlockSpec(memory_space=pl.ANY), pl.BlockSpec(memory_space=pltpu.VMEM)
    out_specs = [near] * len(outs)
    if trades:
        sums = jax.ShapeDtypeStruct(outs[-1].shape, BF16)
        scratch.append(pltpu.VMEM(sums.shape, BF16))
        scratch += [pltpu.SemaphoreType.DMA((len(trades),))] * 2
        outs += [jax.ShapeDtypeStruct(a.shape, a.dtype) for a in traded] + [sums]
        out_specs += [far] * len(traded) + [near]
    return pl.pallas_call(
        functools.partial(scatter_kernel, steps, cuts, len(arrays), lists, tuple(trades)),
        name=name,
        in_specs=[far] * (len(arrays) + len(traded)),
        out_specs=out_specs,
        out_shape=outs,
        scratch_shapes=scratch,
        compiler_params=pltpu.CompilerParams(
            collective_id=collective, has_side_effects=True, vmem_limit_bytes=60 * 2**20
        ),
    )(
        *[a.reshape((2,) * steps + (share, a.shape[1])) for share, a in zip(shares, arrays)],
        *traded,
    )


def body(phonemes, phone_lengths, durations, pitch_bins, energy_bins, joint_weight, output_weight,
         widen_weight, narrow_weight, block_scales, block_shifts, predictor_convs,
         predictor_scales, predictor_shifts, predictor_outputs, pitch_table, energy_table,
         mel_weight, mel_cotangent, duration_cotangent, pitch_cotangent, energy_cotangent):
    first = lax.axis_index(SECTION) == 0
    n = phonemes.shape[0]
    frames = jnp.sum(durations, axis=1)
    block_weights = (joint_weight[0], output_weight[0], widen_weight[0], narrow_weight[0],
                     block_scales[0], block_shifts[0])
    weights = dict(zip(W_NAMES, block_weights))
    cot_duration = jnp.pad(duration_cotangent, ((0, 0), (0, SLOT - PHONES))).reshape(1, n * SLOT)
    cot_frames = jnp.concatenate([pitch_cotangent, energy_cotangent])
    encoded, encoded_lo = section_call(
        "encoder_forward",
        dict(counts=phone_lengths, phonemes=phonemes, **weights),
        dict(encoded=((n, PHONES, D), F32), encoded_lo=((n, PHONES, D), BF16)),
        (encoder_forward_branch(), None),
        smem=names(counts=1),
    )
    arrived = lax.ppermute(encoded_lo, SECTION, [(0, 1)])
    duration, preds, mel_own, mel_away, dencoded, dsent, *grads, pack, pack_far = section_call(
        "predictors_or_decoder",
        dict(
            frames=frames,
            counts=phone_lengths,
            encoded=encoded,
            arrived=arrived,
            durations=durations,
            pitch_bins=pitch_bins,
            energy_bins=energy_bins,
            convs=predictor_convs,
            scales=predictor_scales,
            shifts=predictor_shifts,
            readouts=predictor_outputs,
            pitch_table=pitch_table,
            energy_table=energy_table,
            mel_turned=mel_weight.T,
            mel_cotangent=mel_cotangent.transpose(0, 2, 1),
            cot_duration=cot_duration,
            cot_frames=cot_frames,
            **weights,
        ),
        dict(
            duration_pred=((1, n * SLOT), F32),
            frame_preds=((2 * n, FRAMES), F32),
            mel_own=((n, MELS, FRAMES // 2), F32),
            mel_away=((n, MELS, FRAMES // 2), BF16),
            dencoded=((n, PHONES, D), F32),
            dsent=((n, PHONES, D), BF16),
            **GRADS,
            pack=((D, NEAR_PACK), BF16),
            pack_far=((D, PACK - AT_TABLES), BF16),
        ),
        (predictors_branch(n), decoder_branch(n)),
        smem=names(frames=1, counts=1),
    )
    (pack,) = scattered([pack], "pack_sums", 1, 768, ((0,), ()))
    pack, dsent = lax.optimization_barrier((pack, dsent))
    returned = lax.ppermute(dsent, SECTION, [(1, 0)])
    input_own, input_away, *grads = section_call(
        "encoder_backward",
        dict(
            counts=phone_lengths,
            phonemes=phonemes,
            grad_near=dencoded,
            grad_far=returned,
            **weights,
            **dict(zip(G_NAMES, grads)),
        ),
        dict(
            input_own=((n, PHONES // 2, D), F32),
            input_away=((n, PHONES // 2, D), BF16),
            **GRADS,
        ),
        (encoder_backward_branch(), None),
        smem=names(counts=1),
        kept=G_NAMES,
    )
    sums = dict(zip(G_NAMES, grads))
    order = names(g_widen=1, g_narrow=1, g_joint=1, g_output=1, g_vec=1)
    half, some = FRAMES // 2, PHONES // 2
    duration = duration.reshape(n, SLOT)[:, :PHONES]
    small = jnp.concatenate(
        [
            preds[:, half:],
            jnp.pad(duration[:, some:], ((0, 16 - 3 * n), (0, half - some))),
        ]
    ).astype(BF16)
    sums = scattered(
        [sums[n] for n in order] + [pack_far],
        "block_sums",
        2,
        256,
        (range(5), (5, 0, 1, 2, 3, 4)),
        (pack.astype(BF16), small, input_away, mel_away),
        (0, 0, 0, 1, 1),
    )
    near_pack, small, input_away, mel_away, far_pack = sums[6:]
    own = dict(zip(order, sums))
    return assembled(
        n,
        sums[0].shape[0],
        dict(
            **own,
            pack=pack,
            pack_far=sums[5],
            duration=duration,
            preds=preds,
            mel_own=mel_own,
            input_own=input_own,
            near_pack=near_pack,
            small=small,
            input_away=input_away,
            mel_away=mel_away,
            far_pack=far_pack,
        ),
    )


def assemble_kernel(n, ins, outs, *refs):
    far, refs = refs[: len(ins)], refs[len(ins) :]
    outs_refs, (*near, sem) = refs[: len(outs)], refs[len(outs) :]
    copies = [
        pltpu.make_async_copy(a, b, sem.at[k]) for k, (a, b) in enumerate(zip(far, near))
    ]
    for copy in copies:
        copy.start()
    for copy in copies:
        copy.wait()
    r = Refs(ins + outs, [*near, *outs_refs])
    first = lax.axis_index(SECTION) == 0
    half, some = FRAMES // 2, PHONES // 2

    def choose(near, far):
        return jnp.where(first, near.astype(F32), far.astype(F32))

    for s in range(n):
        r.o_mel[s] = choose(r.mel_away[s], r.mel_own[s])
        r.o_input[s] = choose(r.input_own[s], r.input_away[s])
    preds = choose(r.preds[:, 0:half], r.small[0 : 2 * n, :])
    r.o_pitch[...] = preds[0:n]
    r.o_energy[...] = preds[n : 2 * n]
    r.o_duration[...] = choose(r.duration[:, 0:some], r.small[2 * n : 3 * n, 0:some])
    r.o_joint[0] = r.g_joint[...]
    r.o_output[0] = r.g_output[...]
    r.o_widen[0] = r.g_widen[...]
    r.o_narrow[0] = r.g_narrow[...]
    share = r.pack.shape[0]
    block_vec = r.g_vec[...].T
    vec = choose(r.pack[:, AT_VECTORS:AT_TABLES], r.near_pack[:, AT_VECTORS:AT_TABLES]).T
    for k in range(2):
        r.o_block_scales[0, k : k + 1, :] = block_vec[2 * k : 2 * k + 1, 0:share]
        r.o_block_shifts[0, k : k + 1, :] = block_vec[2 * k + 1 : 2 * k + 2, 0:share]
        for p in range(3):
            at = (2 * p + k) * 3 * D
            r.o_convs[p, k] = choose(
                r.pack[:, at : at + 3 * D], r.near_pack[:, at : at + 3 * D]
            )
            row = 8 * p + 2 * k
            r.o_scales[p, k : k + 1, :] = vec[row : row + 1, 0:share]
            r.o_shifts[p, k : k + 1, :] = vec[row + 1 : row + 2, 0:share]
    for p in range(3):
        r.o_readouts[p : p + 1, :] = vec[8 * p + 4 : 8 * p + 5, 0:share]
    near = choose(r.pack[:, AT_TABLES:], r.near_pack[:, AT_TABLES:])
    far = choose(r.far_pack[...], r.pack_far[...])
    r.o_pitch_table[...] = near + far[:, 0:BINS]
    r.o_energy_table[...] = far[:, BINS : 2 * BINS]
    r.o_mel_weight[...] = far[:, 2 * BINS : 2 * BINS + MELS]


def assembled(n, widen_rows, ins):
    share = ins[names(pack=1)[0]].shape[0]
    narrow_rows = FF * share // D
    outs = dict(
        o_mel=(n, MELS, FRAMES // 2),
        o_duration=(n, PHONES // 2),
        o_pitch=(n, FRAMES // 2),
        o_energy=(n, FRAMES // 2),
        o_input=(n, PHONES // 2, D),
        o_joint=(1, share, 3 * D),
        o_output=(1, share, D),
        o_widen=(1, widen_rows, FF),
        o_narrow=(1, narrow_rows, D),
        o_block_scales=(1, 2, share),
        o_block_shifts=(1, 2, share),
        o_convs=(3, 2, share, 3 * D),
        o_scales=(3, 2, share),
        o_shifts=(3, 2, share),
        o_readouts=(3, share),
        o_pitch_table=(share, BINS),
        o_energy_table=(share, BINS),
        o_mel_weight=(share, MELS),
    )
    whole = pl.BlockSpec(memory_space=pltpu.VMEM)
    results = pl.pallas_call(
        functools.partial(assemble_kernel, n, list(ins), list(outs)),
        name="assemble",
        in_specs=[pl.BlockSpec(memory_space=pl.ANY)] * len(ins),
        out_specs=[whole] * len(outs),
        out_shape=[jax.ShapeDtypeStruct(shape, F32) for shape in outs.values()],
        scratch_shapes=[
            *[pltpu.VMEM(a.shape, a.dtype) for a in ins.values()],
            pltpu.SemaphoreType.DMA((len(ins),)),
        ],
        compiler_params=pltpu.CompilerParams(vmem_limit_bytes=61 * 2**20),
    )(*ins.values())
    results = list(results)
    results[0] = results[0].transpose(0, 2, 1)
    results[11] = results[11].transpose(0, 1, 3, 2)
    results[15], results[16] = results[15].T, results[16].T
    return tuple(results)


def solution(mesh):
    halves_of_rows = P(DP, SECTION)
    row, rows, blocks = P(DP), P(DP, None), P(DP, None, None)
    table, block_sums = P(SECTION, None, None), P(SECTION, DP, None)
    block_vectors, vectors, columns = P(SECTION, None, DP), P(None, None, DP), P(None, DP)
    return jax.shard_map(
        body,
        mesh=mesh,
        in_specs=(blocks, row, rows, rows, rows) + (table,) * 6 + (P(),) * 7
        + (blocks, rows, rows, rows),
        out_specs=(
            P(DP, SECTION, None),
            halves_of_rows,
            halves_of_rows,
            halves_of_rows,
            P(DP, SECTION, None),
            *(block_sums,) * 4,
            block_vectors,
            block_vectors,
            P(None, None, None, DP),
            vectors,
            vectors,
            columns,
            columns,
            columns,
            rows,
        ),
        check_vma=False,
    )
```

profile of v0, /device:TPU:20, one launch (start us, length us, event | category | flops | bytes accessed | tf_op | source)
XLA Modules:
  0.0 271.1 jit_solution(15213827393056235239)
XLA Ops:
  0.7 0.0 copy-start.6
  0.7 0.0 copy-start.3
  0.7 0.0 copy-start.5
  0.7 0.0 copy-start.4
  0.7 0.8 encoder_forward.1
  1.5 1.3 collective-permute-start
  2.8 0.0 copy-done.6
  2.8 0.7 reshape.63.refs_15_
  3.5 0.0 copy-done.3
  3.5 0.6 reduce_sum.9.refs_0_
  4.1 0.0 copy-done.5
  4.1 0.0 copy-done.4
  4.1 0.6 pad_maximum_fusion.refs_16_
  4.8 15.7 %collective-permute-done.refs_3_ = bf16[4,160,256]{2,1,0:T(8,128)(2,1)S(1)} collective-permute-done((bf16[4,160,256]{2,1,0:T(8,128)(2,1)}, bf16[4,160,256]{2,1,0:T(8,128)(2,1)S(1)}, u32[]{:S(2)}, u32[]{:S(2)}) %collective-permute-start) | collective-permute-done | bytes 327712 | tf_op jit(solution)/shard_map/ppermute | solution.py:1127
  20.5 0.0 copy-start.1
  20.5 0.7 copy-done.1
  21.2 155.9 %predictors_or_decoder.1 = (f32[1,768]{1,0:T(1,128)}, f32[8,1024]{1,0:T(8,128)}, f32[4,80,512]{2,1,0:T(8,128)}, bf16[4,80,512]{2,1,0:T(8,128)(2,1)}, f32[4,160,2...) custom-call(s32[4]{0:T(128)} %reduce_sum.9.refs_0_, ...), custom_call_target="tpu_custom_call" | custom-call | tf_op jit(solution)/shard_map/predictors_or_decoder/pallas_call | solution.py:589
  177.2 1.3 pack_sums.1.refs_5_
  178.5 1.3 collective-permute-start.1
  179.8 0.7 reduce
  180.5 0.1 reshape.71
  180.6 0.0 copy-start.2
  180.6 0.1 slice.21
  180.7 0.7 slice.20
  181.4 1.7 convert_element_type.8.refs_6_
  183.0 0.6 fusion.1.refs_7_
  183.7 3.1 %collective-permute-done.1.refs_3_ = bf16[4,160,256]{2,1,0:T(8,128)(2,1)S(1)} collective-permute-done((bf16[4,160,256]{2,1,0:T(8,128)(2,1)}, bf16[4,160,256]{2,1,0:T(8,128)(2,1)S(1)}, u32[]{:S(2)}, u32[]{:S(2)}) %collective-permute-start.1) | collective-permute-done | bytes 327712 | tf_op jit(solution)/shard_map/ppermute | solution.py:1166
  186.8 0.0 copy-start
  186.8 0.7 copy-done
  187.5 0.9 encoder_backward.1
  188.4 0.0 copy-done.2
  188.4 79.1 %block_sums.1 = (f32[144,1024]{1,0:T(8,128)}, f32[64,256]{1,0:T(8,128)}, f32[16,768]{1,0:T(8,128)}, f32[16,256]{1,0:T(8,128)}, f32[16,128]{1,0:T(8,128)}, /*inde...) custom-call(bf16[2,2,2,2,144,1024]{5,4,3,2,1,0:T(8,128)(2,1)} %bitca, ...), custom_call_target="tpu_custom_call" | custom-call | tf_op jit(solution)/shard_map/block_sums/pallas_call | solution.py:1092
  267.6 3.3 %assemble.1 = (f32[4,80,512]{2,1,0:T(8,128)}, f32[4,80]{1,0:T(4,128)}, f32[4,512]{1,0:T(4,128)}, f32[4,512]{1,0:T(4,128)}, f32[4,80,256]{2,1,0:T(8,128)}, /*inde...) custom-call(f32[144,1024]{1,0:T(8,128)} %get-tuple-element.93.refs_0, ...), custom_call_target="tpu_custom_call" | custom-call | tf_op jit(solution)/shard_map/assemble/pallas_call | solution.py:1302
  (1 shorter events, 0.0 us)
Async XLA Ops:
  0.7 2.2 copy-start.6
  0.7 2.8 %copy-start.3 = (s32[4,160]{1,0:T(4,128)S(1)}, s32[4,160]{1,0:T(4,128)}, u32[]{:S(2)}) copy-start(s32[4,160]{1,0:T(4,128)} %refs_4_.1) | copy-start | bytes 7684
  0.7 3.5 %copy-start.5 = (f32[4,1024]{1,0:T(4,128)S(1)}, f32[4,1024]{1,0:T(4,128)}, u32[]{:S(2)}) copy-start(f32[4,1024]{1,0:T(4,128)} %param.42) | copy-start | bytes 49156
  0.7 3.5 %copy-start.4 = (f32[4,1024]{1,0:T(4,128)S(1)}, f32[4,1024]{1,0:T(4,128)}, u32[]{:S(2)}) copy-start(f32[4,1024]{1,0:T(4,128)} %param.43) | copy-start | bytes 49156
  1.5 19.0 %collective-permute-start = (bf16[4,160,256]{2,1,0:T(8,128)(2,1)}, bf16[4,160,256]{2,1,0:T(8,128)(2,1)S(1)}, u32[]{:S(2)}, u32[]{:S(2)}) collective-permute-start(bf16[4,160,256]{2,1,0:T(8,128)(2,1)} %get-tuple-element.72), channel_id=1, source_target_pairs={{0,16},{1,17},{2,18},{3,19},{4,20},{5,21},{6,22},{7,23},{8,24},{9,... | collective-permute-start | bytes 983048 | tf_op jit(solution)/shard_map/ppermute | solution.py:1127
  20.5 0.7 copy-start.1
  178.5 8.3 %collective-permute-start.1 = (bf16[4,160,256]{2,1,0:T(8,128)(2,1)}, bf16[4,160,256]{2,1,0:T(8,128)(2,1)S(1)}, u32[]{:S(2)}, u32[]{:S(2)}) collective-permute-start(bf16[4,160,256]{2,1,0:T(8,128)(2,1)} %get-tuple-element.76), channel_id=1, source_target_pairs={{16,0},{17,1},{18,2},{19,3},{20,4},{21,5},{22,6},{23,7},{24,8},{25... | collective-permute-start | bytes 983048 | tf_op jit(solution)/shard_map/ppermute | solution.py:1166
  180.6 7.8 %copy-start.2 = (f32[4,192]{1,0:T(4,128)}, f32[4,192]{1,0:T(4,128)S(1)}, u32[]{:S(2)}) copy-start(f32[4,192]{1,0:T(4,128)S(1)} %reshape.71) | copy-start | bytes 9220
  186.8 0.7 copy-start
where the time goes:
time: 277 us; the launch traced here: 271 us
  Pallas kernels  241 us (87%)
  waiting for transfers between devices  18.9 us (7%)
  other arithmetic  4.21 us (2%)
  local copies, waits for them, and re-layouts  3.01 us (1%)
    pallas_call x3, Pallas kernels, section_call(): pl.pallas_call(kernel, name=name, in_specs=[pl.BlockSpec(memory_space=plt...  158 us
    pallas_call x2, Pallas kernels, scattered(): pl.pallas_call(functools.partial(scatter_kernel, steps, cuts, len(arrays)...  80.5 us
    ppermute x1, waiting for transfers between devices, body(): arrived = lax.ppermute(encoded_lo, SECTION, [(0, 1)])  15.7 us
  transfers between devices with their start and end apart: 2, of which 2 were waited for; matrix products, arithmetic and copies ran while one was open for 2% of the time, Pallas kernels for 0%

commit v1 on v0

--- a/solution.py
+++ b/solution.py
@@ -301,12 +301,9 @@
 
 
 def ffn_weight_grads(b, length):
-    def widen(t, _):
-        at = aligned(t, 3 * D)
+    for t in range(3):
+        at = slice(t * 3 * D, (t + 1) * 3 * D)
         b.a_widen[at, :] += dot_tn(b.cols[0:length, at], b.dwid[0:length, :])
-        return 0
-
-    lax.fori_loop(0, 3, widen, 0)
     b.a_narrow[...] += dot_tn(b.act[0:length, :], b.dnar[0:length, :])
 
 
@@ -496,7 +493,6 @@
             b.h_lo[rows, :] = adapted.astype(BF16)
         attention_forward(layout, b, w, counts, length)
         b.first[length + 8 : length + 16, :] = jnp.zeros((8, D), F32)
-        pl.when(s == 0)(lambda: wait_weights(b, w))
         ffn_forward(b, w, length)
         for r0, size in tiles:
             rows = slice(r0, r0 + size)
@@ -514,7 +510,6 @@
             second_norm_back(b, w, r0, size, dy, n, rstd)
         ffn_backward(b, w, length)
         ffn_weight_grads(b, length)
-        pl.when(s == sequences - 1)(lambda: send_large_grads(b, o))
 
         def finish(_, at, q, dh):
             b.datt[at : at + q, :] = dh.astype(BF16)
@@ -527,7 +522,9 @@
     def one(s):
         sequence(s, FRAMES)
 
+    wait_weights(b, w)
     each(sequences, one)
+    send_large_grads(b, o)
     store_block_grads(b, o)
     r.pack_far[:, 0 : 2 * BINS] = r.a_table[...].T.astype(BF16)
     r.pack_far[:, 2 * BINS :] = jnp.zeros((D, 128), BF16)
@@ -873,6 +870,13 @@
         r.dencoded[s] = r.dencoded[s] + dencoded[0:PHONES]
 
     each(sequences, one)
+    some = PHONES // 2
+    r.away[...] = jnp.zeros_like(r.away)
+    r.away[0 : 2 * sequences, :] = r.frame_preds[:, FRAMES // 2 :]
+    for s in range(sequences):
+        line = r.duration_pred[:, s * SLOT + some : s * SLOT + PHONES]
+        r.away[2 * sequences + s : 2 * sequences + s + 1, 0:some] = line
+    r.small[...] = r.away[...].astype(BF16)
     for p in range(3):
         for k in range(2):
             at = (2 * p + k) * 3 * D
@@ -887,8 +891,9 @@
         functools.partial(predictor_kernel, sequences),
         names(frames=1, counts=1, encoded=1, durations=1, pitch_bins=1, convs=1, scales=1,
               shifts=1, readouts=1, pitch_table=1, cot_duration=1, cot_frames=1),
-        names(duration_pred=1, frame_preds=1, dencoded=1, pack=1),
+        names(duration_pred=1, frame_preds=1, small=1, dencoded=1, pack=1),
         dict(
+            away=pltpu.VMEM((16, FRAMES // 2), F32),
             a_conv=pltpu.VMEM((3, 2, D, 3 * D), F32),
             a_vec=pltpu.VMEM((3, 8, D), F32),
             a_table=pltpu.VMEM((BINS, D), F32),
@@ -931,9 +936,9 @@
     return out
 
 
-def scatter_kernel(steps, cuts, count, lists, trades, *refs):
+def scatter_kernel(steps, cuts, count, lists, trades, given, *refs):
     n, m = len(cuts), len(trades)
-    given = max(m - 1, 0)
+    late = given < m
     sources, refs = refs[:count], refs[count:]
     traded, refs = refs[:given], refs[given:]
     outs, refs = refs[:count], refs[count:]
@@ -941,7 +946,9 @@
     mine, landed = refs[:n], refs[n : n * (1 + steps)]
     load_sem, send_sem, recv_sem, *rest = refs[n * (1 + steps) :]
     if m:
-        rounded, trade_send, trade_recv = rest
+        trade_send, trade_recv = rest[:2]
+    if late:
+        rounded = rest[2]
         traded = traded + (rounded,)
     me = lax.axis_index(DP)
     bits = [lax.rem(lax.div(me, 1 << k), 2) for k in range(steps)]
@@ -1005,18 +1012,18 @@
 
     def run(section, chosen):
         barrier = pltpu.get_barrier_semaphore()
-        for partner in partners:
+        for partner in partners if chosen else ():
             pl.semaphore_signal(
                 barrier, inc=1, device_id={DP: partner}, device_id_type=pl.DeviceIdType.MESH
             )
-        if m:
+        if any(sender != section for sender in trades):
             pl.semaphore_signal(
                 barrier,
                 inc=1,
                 device_id={SECTION: 1 - lax.axis_index(SECTION)},
                 device_id_type=pl.DeviceIdType.MESH,
             )
-        pl.semaphore_wait(barrier, steps + (1 if m else 0))
+        pl.semaphore_wait(barrier, (steps if chosen else 0) + (1 if section in trades else 0))
         size = len(chosen)
         for i in range(given):
             if trades[i] == section:
@@ -1029,7 +1036,7 @@
                 at = turn - k
                 if 0 <= at < size:
                     finish(chosen[at], k)
-                    if m and trades[-1] == section and k == steps - 1 and at == last[-1]:
+                    if late and trades[-1] == section and k == steps - 1 and at == last[-1]:
                         rounded[...] = outs[count - 1][...].astype(BF16)
                         trade(m - 1).start()
         for i in chosen:
@@ -1042,7 +1049,7 @@
                 trade(i).wait_recv()
 
     for section, chosen in enumerate(lists):
-        if chosen:
+        if chosen or m:
             here = (lax.axis_index(SECTION) == section).astype(jnp.int32)
             each(here, functools.partial(one_time, run, section, chosen))
 
@@ -1051,12 +1058,12 @@
     run(section, chosen)
 
 
-def scattered(arrays, name, collective, width, parts, traded=(), trades=()):
+def scattered(arrays, name, collective, width, parts, traded, trades):
     ways = lax.axis_size(DP)
     steps = ways.bit_length() - 1
     if ways != 1 << steps or any(a.shape[0] // ways % 16 for a in arrays):
         sums = scattered_anyhow(arrays)
-        traded = [*traded, sums[-1].astype(BF16)] if trades else []
+        traded = [*traded, sums[-1].astype(BF16)]
         return sums + [
             lax.ppermute(a, SECTION, [(s, 1 - s)]) for a, s in zip(traded, trades)
         ]
@@ -1083,14 +1090,18 @@
     outs = [jax.ShapeDtypeStruct((share, a.shape[1]), F32) for share, a in zip(shares, arrays)]
     far, near = pl.BlockSpec(memory_space=pl.ANY), pl.BlockSpec(memory_space=pltpu.VMEM)
     out_specs = [near] * len(outs)
-    if trades:
-        sums = jax.ShapeDtypeStruct(outs[-1].shape, BF16)
+    scratch += [pltpu.SemaphoreType.DMA((len(trades),))] * 2
+    sums = jax.ShapeDtypeStruct(outs[-1].shape, BF16)
+    outs += [jax.ShapeDtypeStruct(a.shape, a.dtype) for a in traded]
+    out_specs += [far] * len(traded)
+    if len(trades) > len(traded):
         scratch.append(pltpu.VMEM(sums.shape, BF16))
-        scratch += [pltpu.SemaphoreType.DMA((len(trades),))] * 2
-        outs += [jax.ShapeDtypeStruct(a.shape, a.dtype) for a in traded] + [sums]
-        out_specs += [far] * len(traded) + [near]
+        outs.append(sums)
+        out_specs.append(near)
     return pl.pallas_call(
-        functools.partial(scatter_kernel, steps, cuts, len(arrays), lists, tuple(trades)),
+        functools.partial(
+            scatter_kernel, steps, cuts, len(arrays), lists, tuple(trades), len(traded)
+        ),
         name=name,
         in_specs=[far] * (len(arrays) + len(traded)),
         out_specs=out_specs,
@@ -1125,7 +1136,7 @@
         smem=names(counts=1),
     )
     arrived = lax.ppermute(encoded_lo, SECTION, [(0, 1)])
-    duration, preds, mel_own, mel_away, dencoded, dsent, *grads, pack, pack_far = section_call(
+    duration, preds, small, mel_own, mel_away, dencoded, dsent, *grads, pack, pack_far = section_call(
         "predictors_or_decoder",
         dict(
             frames=frames,
@@ -1150,6 +1161,7 @@
         dict(
             duration_pred=((1, n * SLOT), F32),
             frame_preds=((2 * n, FRAMES), F32),
+            small=((16, FRAMES // 2), BF16),
             mel_own=((n, MELS, FRAMES // 2), F32),
             mel_away=((n, MELS, FRAMES // 2), BF16),
             dencoded=((n, PHONES, D), F32),
@@ -1161,9 +1173,7 @@
         (predictors_branch(n), decoder_branch(n)),
         smem=names(frames=1, counts=1),
     )
-    (pack,) = scattered([pack], "pack_sums", 1, 768, ((0,), ()))
-    pack, dsent = lax.optimization_barrier((pack, dsent))
-    returned = lax.ppermute(dsent, SECTION, [(1, 0)])
+    pack, returned = scattered([pack], "pack_sums", 1, 768, ((0,), ()), (dsent,), (1,))
     input_own, input_away, *grads = section_call(
         "encoder_backward",
         dict(
@@ -1185,21 +1195,13 @@
     )
     sums = dict(zip(G_NAMES, grads))
     order = names(g_widen=1, g_narrow=1, g_joint=1, g_output=1, g_vec=1)
-    half, some = FRAMES // 2, PHONES // 2
-    duration = duration.reshape(n, SLOT)[:, :PHONES]
-    small = jnp.concatenate(
-        [
-            preds[:, half:],
-            jnp.pad(duration[:, some:], ((0, 16 - 3 * n), (0, half - some))),
-        ]
-    ).astype(BF16)
     sums = scattered(
         [sums[n] for n in order] + [pack_far],
         "block_sums",
         2,
-        256,
+        128,
         (range(5), (5, 0, 1, 2, 3, 4)),
-        (pack.astype(BF16), small, input_away, mel_away),
+        (pack, small, input_away, mel_away),
         (0, 0, 0, 1, 1),
     )
     near_pack, small, input_away, mel_away, far_pack = sums[6:]
@@ -1244,10 +1246,14 @@
     for s in range(n):
         r.o_mel[s] = choose(r.mel_away[s], r.mel_own[s])
         r.o_input[s] = choose(r.input_own[s], r.input_away[s])
-    preds = choose(r.preds[:, 0:half], r.small[0 : 2 * n, :])
+    small = r.small[...].astype(F32)
+    preds = choose(r.preds[:, 0:half], small[0 : 2 * n, :])
     r.o_pitch[...] = preds[0:n]
     r.o_energy[...] = preds[n : 2 * n]
-    r.o_duration[...] = choose(r.duration[:, 0:some], r.small[2 * n : 3 * n, 0:some])
+    for s in range(n):
+        r.o_duration[s : s + 1, :] = choose(
+            r.duration[:, s * SLOT : s * SLOT + some], small[2 * n + s : 2 * n + s + 1, 0:some]
+        )
     r.o_joint[0] = r.g_joint[...]
     r.o_output[0] = r.g_output[...]
     r.o_widen[0] = r.g_widen[...]

time: 277 us -> 266 us (0.960)
  the two profiles are of different devices: /device:TPU:20 before, /device:TPU:0 now
where the time goes in v1:
time: 266 us; the launch traced here: 261 us
  Pallas kernels  249 us (94%)
  waiting for transfers between devices  6.21 us (2%)
    pallas_call x3, Pallas kernels, section_call(): pl.pallas_call(kernel, name=name, in_specs=[pl.BlockSpec(memory_space=plt...  128 us
    pallas_call x2, Pallas kernels, scattered(): pl.pallas_call(functools.partial(scatter_kernel, steps, cuts, len(arrays)...  118 us
    ppermute x1, waiting for transfers between devices, body(): arrived = lax.ppermute(encoded_lo, SECTION, [(0, 1)])  6.21 us
  transfers between devices with their start and end apart: 1, of which 1 were waited for; matrix products, arithmetic and copies ran while one was open for 1% of the time, Pallas kernels for 0%

profile of v1, /device:TPU:0, one launch (start us, length us, event | category | flops | bytes accessed | tf_op | source)
XLA Modules:
  0.0 260.6 jit_solution(5994489245269397539)
XLA Ops:
  0.7 0.0 copy-start.4
  0.7 0.0 copy-start.1
  0.7 0.0 copy-start.2
  0.7 0.0 copy-start.3
  0.7 10.1 %encoder_forward.1 = (f32[4,160,256]{2,1,0:T(8,128)}, bf16[4,160,256]{2,1,0:T(8,128)(2,1)}) custom-call(s32[4]{0:T(128)} %refs_0_.3, bf16[4,160,256]{2,1,0:T(8,128)(2,1)} %refs_1_.5, bf16[256,768]{1,0:T(8,128)(2,1)} %bitcast.26, bf16[256,256]{1,0:T(8,128)(2,1)} %bitcast.32, bf16[2304,1024]{1,0:T(8,128)(2,1)} %bitcast.19, bf16[1024,256]{1,0:T(8,128)(2,1)} %bitcast.23, ...), custom_call_target="tpu_custom_call" | custom-call | tf_op jit(solution)/shard_map/encoder_forward/pallas_call | solution.py:586
  10.8 1.3 collective-permute-start
  12.1 0.0 copy-done.4
  12.1 0.7 reshape.60.refs_15_
  12.8 0.0 copy-done.1
  12.8 0.6 reduce_sum.9.refs_0_
  13.4 0.0 copy-done.2
  13.4 0.0 copy-done.3
  13.4 0.6 pad_maximum_fusion.refs_16_
  14.1 6.2 %collective-permute-done.refs_3_ = bf16[4,160,256]{2,1,0:T(8,128)(2,1)S(1)} collective-permute-done((bf16[4,160,256]{2,1,0:T(8,128)(2,1)}, bf16[4,160,256]{2,1,0:T(8,128)(2,1)S(1)}, u32[]{:S(2)}, u32[]{:S(2)}) %collective-permute-start) | collective-permute-done | bytes 327712 | tf_op jit(solution)/shard_map/ppermute | solution.py:1138
  20.3 0.0 copy-start
  20.3 0.7 copy-done
  21.0 94.6 %predictors_or_decoder.1 = (f32[1,768]{1,0:T(1,128)}, f32[8,1024]{1,0:T(8,128)}, bf16[16,512]{1,0:T(8,128)(2,1)}, f32[4,80,512]{2,1,0:T(8,128)}, bf16[4,80,512]{...) custom-call(s32[4]{0:T(128)} %reduce_sum.9.refs_0_, ...), custom_call_target="tpu_custom_call" | custom-call | tf_op jit(solution)/shard_map/predictors_or_decoder/pallas_call | solution.py:586
  115.6 66.6 %pack_sums.1 = (f32[16,4992]{1,0:T(8,128)}, bf16[4,160,256]{2,1,0:T(8,128)(2,1)}) custom-call(bf16[2,2,2,2,16,4992]{5,4,3,2,1,0:T(8,128)(2,1)} %bitcast.29, bf16[4,160,256]{2,1,0:T(8,128)(2,1)} %get-tuple-element.76.refs_1_), custom_call_target="tpu_custom_call" | custom-call | tf_op jit(solution)/shard_map/pack_sums/pallas_call | solution.py:1101
  182.2 23.1 %encoder_backward.1 = (f32[4,80,256]{2,1,0:T(8,128)}, bf16[4,80,256]{2,1,0:T(8,128)(2,1)}, bf16[256,768]{1,0:T(8,128)(2,1)}, bf16[256,256]{1,0:T(8,128)(2,1)}, b...) custom-call(s32[4]{0:T(128)} %refs_0_.3, ...), custom_call_target="tpu_custom_call", output_to_operand_aliasing={{2}: (10, {}), {3}: (11, {}), {4}: (12, {}), {5}: (13, {}),... | custom-call | tf_op jit(solution)/shard_map/encoder_backward/pallas_call | solution.py:586
  205.3 51.7 %block_sums.1 = (f32[144,1024]{1,0:T(8,128)}, f32[64,256]{1,0:T(8,128)}, f32[16,768]{1,0:T(8,128)}, f32[16,256]{1,0:T(8,128)}, f32[16,128]{1,0:T(8,128)}, /*inde...) custom-call(bf16[2,2,2,2,144,1024]{5,4,3,2,1,0:T(8,128)(2,1)} %bitca, ...), custom_call_target="tpu_custom_call" | custom-call | tf_op jit(solution)/shard_map/block_sums/pallas_call | solution.py:1101
  257.0 3.4 %assemble.1 = (f32[4,80,512]{2,1,0:T(8,128)}, f32[4,80]{1,0:T(4,128)}, f32[4,512]{1,0:T(4,128)}, f32[4,512]{1,0:T(4,128)}, f32[4,80,256]{2,1,0:T(8,128)}, /*inde...) custom-call(f32[144,1024]{1,0:T(8,128)} %get-tuple-element.93.refs_0, ...), custom_call_target="tpu_custom_call" | custom-call | tf_op jit(solution)/shard_map/assemble/pallas_call | solution.py:1308
  (1 shorter events, 0.0 us)
Async XLA Ops:
  0.7 11.5 %copy-start.4 = (f32[4,160]{1,0:T(4,128)S(1)}, f32[4,160]{1,0:T(4,128)}, u32[]{:S(2)}) copy-start(f32[4,160]{1,0:T(4,128)} %param.41) | copy-start | bytes 7684
  0.7 12.1 %copy-start.1 = (s32[4,160]{1,0:T(4,128)S(1)}, s32[4,160]{1,0:T(4,128)}, u32[]{:S(2)}) copy-start(s32[4,160]{1,0:T(4,128)} %refs_4_.1) | copy-start | bytes 7684
  0.7 12.8 %copy-start.2 = (f32[4,1024]{1,0:T(4,128)S(1)}, f32[4,1024]{1,0:T(4,128)}, u32[]{:S(2)}) copy-start(f32[4,1024]{1,0:T(4,128)} %param.43) | copy-start | bytes 49156
  0.7 12.7 %copy-start.3 = (f32[4,1024]{1,0:T(4,128)S(1)}, f32[4,1024]{1,0:T(4,128)}, u32[]{:S(2)}) copy-start(f32[4,1024]{1,0:T(4,128)} %param.42) | copy-start | bytes 49156
  10.8 9.5 %collective-permute-start = (bf16[4,160,256]{2,1,0:T(8,128)(2,1)}, bf16[4,160,256]{2,1,0:T(8,128)(2,1)S(1)}, u32[]{:S(2)}, u32[]{:S(2)}) collective-permute-start(bf16[4,160,256]{2,1,0:T(8,128)(2,1)} %get-tuple-element.73), channel_id=1, source_target_pairs={{0,16},{1,17},{2,18},{3,19},{4,20},{5,21},{6,22},{7,23},{8,24},{9,... | collective-permute-start | bytes 983048 | tf_op jit(solution)/shard_map/ppermute | solution.py:1138
  20.3 0.7 copy-start
